TPU v7x, 512 devices: a whole 4x8x8 slice. The times are simulated.
512 devices in a mesh: inst: 2 (over y_hi), blk: 256 (over z, y_lo, x, core).
Axes of the slice: x: 4, y: 8 (y_hi: 2, y_lo: 4; y = y_hi * 4 + y_lo), z: 8, core: 2. Of those that a mesh axis runs over, the one named last changes fastest.
Arguments:
- state: float32 [8, 5, 256, 32, 256], P('inst', None, 'blk'), as said below
- slot_of: int32 [256], replicated, may hold values from 0 to 255, as said below
- conn_block: int32 [256, 2], replicated, may hold values from 0 to 255, as said below
- conn_side: int32 [256, 2], replicated, may hold values from 0 to 1
- conn_shift: int32 [256, 2], replicated, may hold values from 0 to 255
- rows: int32 [256], replicated, may hold values from 16 to 32
Outputs:
- residual: float32 [8, 5, 256, 32, 256], P('inst', None, 'blk')
Inputs may be any that keep to these rules, and one draw needn't show every extreme that they name: slot_of is a permutation of the block numbers. With d(b) = slot_of[b], the index along blk of the device holding block b, d(conn_block[b, f]) - d(b) taken cyclically modulo the number of blk devices lies within -2 to 2; both ends are reached in every draw. `state`: density and pressure are positive.
All inputs are finite; a program needn't handle non-finite values.
Results may differ from a plain program's by a relative error of at most 0.00012.
Values sent between devices are 32-bit elements; how exact they have to be, the bound alone decides.
A program may use at most 64 MiB of HBM per device.

v0:
```python
import math
import jax
import jax.numpy as jnp
from jax import lax
from jax.sharding import PartitionSpec as P

REACH = 2
GAMMA_MINUS = 0.4
DAMPING = 0.05
FREQUENCY = 1.0


def passed_along(value, axis, steps):
    count = lax.axis_size(axis)
    pairs = [(source, (source + steps) % count) for source in range(count)]
    return lax.ppermute(value, axis, pairs)


def spectral_matrix(count):
    position = jnp.arange(count, dtype=jnp.int32)
    offset = position[:, None] - position[None, :]
    angle = math.pi / count * offset.astype(jnp.float32)
    safe_sin = jnp.where(offset == 0, 1.0, jnp.sin(angle))
    parity = 1.0 - 2.0 * jnp.mod(offset, 2).astype(jnp.float32)
    return jnp.where(offset == 0, 0.0, 0.5 * FREQUENCY * parity * jnp.cos(angle) / safe_sin)


def euler_flux(fields, direction):
    density = fields[:, 0]
    momentum_x = fields[:, 1]
    momentum_y = fields[:, 2]
    momentum_z = fields[:, 3]
    energy = fields[:, 4]
    pressure = GAMMA_MINUS * (
        energy
        - 0.5
        * (momentum_x * momentum_x + momentum_y * momentum_y + momentum_z * momentum_z)
        / density
    )
    velocity = fields[:, direction] / density
    parts = [
        fields[:, direction],
        momentum_x * velocity,
        momentum_y * velocity,
        momentum_z * velocity,
        (energy + pressure) * velocity,
    ]
    parts[direction] = parts[direction] + pressure
    return jnp.stack(parts, axis=1)


def edge_rows(state, my_rows):
    low = state[:, :, :, 0:2]
    upper = lax.dynamic_slice_in_dim(state[:, :, 0], my_rows[0] - 2, 2, 2)
    highs = [upper[:, :, ::-1]]
    high = jnp.stack(highs, axis=2)
    return jnp.stack([low, high], axis=3)


def pick_ghosts(all_rims, local_slot, nb_side, shift):
    faces = []
    for face in range(2):
        taken = lax.dynamic_index_in_dim(all_rims, local_slot[0, face], 2, keepdims=False)
        taken = lax.dynamic_index_in_dim(taken, nb_side[0, face], 2, keepdims=False)
        faces.append(jnp.roll(taken, -shift[0, face], axis=3))
    per_block = [jnp.stack(faces, axis=2)]
    return jnp.stack(per_block, axis=2)


def spatial_residual(fields, ghosts, block_rows):
    row_count = fields.shape[3]
    stacked = jnp.concatenate([ghosts[:, :, :, 0, ::-1], fields, fields[:, :, :, -2:]], axis=3)
    offset = jnp.arange(row_count + 4, dtype=jnp.int32)[None, :] - 2 - block_rows[:, None]
    first_layer = (offset == 0)[None, None, :, :, None]
    second_layer = (offset == 1)[None, None, :, :, None]
    extended = jnp.where(
        first_layer,
        ghosts[:, :, :, 1, 0][:, :, :, None],
        jnp.where(second_layer, ghosts[:, :, :, 1, 1][:, :, :, None], stacked),
    )
    flux_rows = euler_flux(extended, 1)
    slope_rows = (
        8.0 * (flux_rows[:, :, :, 3:-1] - flux_rows[:, :, :, 1:-3])
        - (flux_rows[:, :, :, 4:] - flux_rows[:, :, :, :-4])
    ) / 12.0
    smooth_rows = (
        extended[:, :, :, 4:]
        - 4.0 * extended[:, :, :, 3:-1]
        + 6.0 * extended[:, :, :, 2:-2]
        - 4.0 * extended[:, :, :, 1:-3]
        + extended[:, :, :, :-4]
    )
    flux_cols = euler_flux(fields, 2)
    slope_cols = (
        8.0 * (jnp.roll(flux_cols, -1, 4) - jnp.roll(flux_cols, 1, 4))
        - (jnp.roll(flux_cols, -2, 4) - jnp.roll(flux_cols, 2, 4))
    ) / 12.0
    smooth_cols = (
        jnp.roll(fields, -2, 4)
        - 4.0 * jnp.roll(fields, -1, 4)
        + 6.0 * fields
        - 4.0 * jnp.roll(fields, 1, 4)
        + jnp.roll(fields, 2, 4)
    )
    return -(slope_rows + slope_cols) - DAMPING * (smooth_rows + smooth_cols)


def on_device(state, slot_of, conn_block, conn_side, conn_shift, rows):
    inst_dev = state.shape[0]
    blk_dev = state.shape[2]
    row_count = state.shape[3]
    blocks = slot_of.shape[0]
    ids_of_slot = (
        jnp.zeros((blocks,), jnp.int32).at[slot_of].set(jnp.arange(blocks, dtype=jnp.int32))
    )
    blk_place = lax.axis_index("blk")
    my_slots = blk_place * blk_dev + jnp.arange(blk_dev, dtype=jnp.int32)
    my_ids = ids_of_slot[my_slots]
    my_rows = rows[my_ids]
    boundary = edge_rows(state, my_rows)
    nb_slots = slot_of[conn_block[my_ids]]
    blk_span = lax.axis_size("blk")
    pieces = []
    for window in range(2 * REACH + 1):
        if window == REACH:
            pieces.append(boundary)
        else:
            pieces.append(passed_along(boundary, "blk", REACH - window))
    all_rims = jnp.concatenate(pieces, axis=2)
    distance = jnp.mod(nb_slots // blk_dev - blk_place + REACH, blk_span)
    local_slot = distance * blk_dev + jnp.mod(nb_slots, blk_dev)
    ghosts = pick_ghosts(all_rims, local_slot, conn_side[my_ids], conn_shift[my_ids])
    spatial = spatial_residual(state, ghosts, my_rows)
    cycle_size = lax.axis_size("inst")
    cycle_place = lax.axis_index("inst")
    derivative = spectral_matrix(inst_dev * cycle_size)
    own_rows = lax.dynamic_slice_in_dim(derivative, cycle_place * inst_dev, inst_dev, 0)
    all_states = lax.all_gather(state, "inst", axis=0, tiled=True)
    source = jnp.einsum("nm,mvbij->nvbij", own_rows, all_states, precision=lax.Precision.HIGHEST)
    inside = (jnp.arange(row_count, dtype=jnp.int32)[None, :] < my_rows[:, None])[
        None, None, :, :, None
    ]
    return jnp.where(inside, spatial - source, 0.0)


def solution(mesh):
    in_specs = (P("inst", None, "blk", None, None), P(), P(), P(), P(), P())
    out_specs = P("inst", None, "blk", None, None)
    return jax.shard_map(
        on_device, mesh=mesh, in_specs=in_specs, out_specs=out_specs, check_vma=False
    )
```

profile of v0, /device:TPU:9, one launch (start us, length us, event | category | flops | bytes accessed | tf_op | source)
XLA Modules:
  0.0 100.9 jit_solution(9239169802677168952)
XLA Ops:
  6.5 0.0 all-gather.2.cloned.1.call-start
  6.6 0.7 compare_select_fusion
  7.3 1.4 %scatter_custom_fusion = s32[256]{0:T(256)S(1)} fusion(s32[256]{0:T(256)S(1)} %compare_select_fusion, s32[256]{0:T(256)S(1)} %iota.25, s32[]{:T(128)} %constant.170.clone.1), kind=kCustom, calls=%fused_computation.104 | custom fusion | bytes 1028 | tf_op jit(solution)/shard_map/scatter | solution.py:114
  8.7 0.7 dynamic-slice.18
  11.5 1.3 %dynamic-slice.19 = s32[1]{0:T(128)} dynamic-slice(s32[256]{0:T(256)} %param.13, s32[]{:T(128)} %bitcast.2), dynamic_slice_sizes={1} | dynamic-slice | bytes 12 | tf_op jit(solution)/shard_map/gather | solution.py:119
  13.9 1.0 %slice_bitcast_fusion = (f32[4,5,1,1,2,256]{5,4,1,0,3,2:T(2,128)S(1)}, f32[4,5,2,256]{3,2,1,0:T(2,128)S(1)}) fusion(f32[4,5,1,32,256]{4,3,2,1,0:T(8,128)} %param.8, s32[]{:T(128)S(6)} %select_n.131), kind=kLoop, calls=%fused_computation.65 | loop fusion | bytes 163844 | tf_op jit(solution)/shard_map/stack | solution.py:57
  14.9 0.2 rev.6
  15.2 3.2 %collective-permute-start = (f32[4,5,1,2,2,256]{5,4,1,0,3,2:T(2,128)S(1)}, f32[4,5,1,2,2,256]{5,4,1,0,3,2:T(2,128)S(1)}, u32[]{:S(2)}, u32[]{:S(2)}) collective-permute-start(f32[4,5,1,2,2,256]{5,4,1,0,3,2:T(2,128)S(1)} %pad_maximum_fusion), channel_id=1, source_target_pairs={{0,2},{1,3},{2,4},{3,5},{4,6},{5,7},{6,8},{7,9},{8,10},{9,11},{10,... | collective-permute-start | bytes 245768 | tf_op jit(solution)/shard_map/ppermute | solution.py:16
  18.4 3.9 %collective-permute-start.1 = (f32[4,5,1,2,2,256]{5,4,1,0,3,2:T(2,128)S(1)}, f32[4,5,1,2,2,256]{5,4,1,0,3,2:T(2,128)S(1)}, u32[]{:S(2)}, u32[]{:S(2)}) collective-permute-start(f32[4,5,1,2,2,256]{5,4,1,0,3,2:T(2,128)S(1)} %pad_maximum_fusion), channel_id=1, source_target_pairs={{0,1},{1,2},{2,3},{3,4},{4,5},{5,6},{6,7},{7,8},{8,9},{9,10},{10,1... | collective-permute-start | bytes 245768 | tf_op jit(solution)/shard_map/ppermute | solution.py:16
  22.3 1.9 %collective-permute-start.2 = (f32[4,5,1,2,2,256]{5,4,1,0,3,2:T(2,128)S(1)}, f32[4,5,1,2,2,256]{5,4,1,0,3,2:T(2,128)S(1)}, u32[]{:S(2)}, u32[]{:S(2)}) collective-permute-start(f32[4,5,1,2,2,256]{5,4,1,0,3,2:T(2,128)S(1)} %pad_maximum_fusion), channel_id=1, source_target_pairs={{0,255},{1,0},{2,1},{3,2},{4,3},{5,4},{6,5},{7,6},{8,7},{9,8},{10,... | collective-permute-start | bytes 245768 | tf_op jit(solution)/shard_map/ppermute | solution.py:16
  24.2 4.3 %collective-permute-start.3 = (f32[4,5,1,2,2,256]{5,4,1,0,3,2:T(2,128)S(1)}, f32[4,5,1,2,2,256]{5,4,1,0,3,2:T(2,128)S(1)}, u32[]{:S(2)}, u32[]{:S(2)}) collective-permute-start(f32[4,5,1,2,2,256]{5,4,1,0,3,2:T(2,128)S(1)} %pad_maximum_fusion), channel_id=1, source_target_pairs={{0,254},{1,255},{2,0},{3,1},{4,2},{5,3},{6,4},{7,5},{8,6},{9,7},{1... | collective-permute-start | bytes 245768 | tf_op jit(solution)/shard_map/ppermute | solution.py:16
  28.5 0.0 all-gather.2.cloned.1.call-update
  28.6 0.2 fusion.45
  28.8 0.6 gather_fusion
  29.4 0.7 fusion.62
  32.7 0.1 constant_dynamic-slice_fusion
  32.7 0.6 fusion.60
  36.0 0.6 fusion.61
  37.9 0.6 fusion.50
  38.5 0.4 copy.48
  38.9 0.0 copy-start.2
  39.0 0.1 multiply_dynamic-update-slice_fusion.5
  39.0 0.1 add_dynamic-update-slice_fusion.1
  39.2 0.1 multiply_dynamic-update-slice_fusion.3
  39.3 0.4 fusion.57
  39.7 1.5 %fusion.59 = (f32[4,5,1,32,255]{4,0,3,1,2:T(4,128)}, f32[4,5,1,32,255]{4,0,3,1,2:T(4,128)}) fusion(f32[4,5,1,32,256]{4,0,3,1,2:T(4,128)S(1)} %multiply_dynamic-update-slice_fusion.3), kind=kLoop, calls=%fused_computation.116 | loop fusion | bytes 2611200 | tf_op jit(solution)/shard_map/jit(_roll_static)/slice | solution.py:95
  41.3 1.1 %fusion.56 = (f32[4,5,1,32,2]{4,0,3,1,2:T(4,128)}, f32[4,5,1,32,2]{4,0,3,1,2:T(4,128)}) fusion(f32[4,5,1,32,256]{4,0,3,1,2:T(4,128)S(1)} %multiply_dynamic-update-slice_fusion.3), kind=kLoop, calls=%fused_computation.113 | loop fusion | bytes 20480 | tf_op jit(solution)/shard_map/jit(_roll_static)/slice | solution.py:96
  42.3 1.0 %fusion.58 = (f32[4,5,1,32,1]{4,0,3,1,2:T(4,128)}, f32[4,5,1,32,1]{4,0,3,1,2:T(4,128)}) fusion(f32[4,5,1,32,256]{4,0,3,1,2:T(4,128)S(1)} %multiply_dynamic-update-slice_fusion.3), kind=kLoop, calls=%fused_computation.115 | loop fusion | bytes 10240 | tf_op jit(solution)/shard_map/jit(_roll_static)/slice | solution.py:95
  43.3 1.5 %fusion.53 = (f32[4,5,1,32,254]{4,0,3,1,2:T(4,128)}, f32[4,5,1,32,254]{4,0,3,1,2:T(4,128)}) fusion(f32[4,5,1,32,256]{4,0,3,1,2:T(4,128)S(1)} %copy.48), kind=kLoop, calls=%fused_computation.110 | loop fusion | bytes 2600960 | tf_op jit(solution)/shard_map/jit(_roll_static)/slice | solution.py:103
  44.9 1.5 %fusion.55 = (f32[4,5,1,32,255]{4,0,3,1,2:T(4,128)}, f32[4,5,1,32,255]{4,0,3,1,2:T(4,128)}) fusion(f32[4,5,1,32,256]{4,0,3,1,2:T(4,128)S(1)} %copy.48), kind=kLoop, calls=%fused_computation.112 | loop fusion | bytes 2611200 | tf_op jit(solution)/shard_map/jit(_roll_static)/slice | solution.py:102
  46.4 1.1 %fusion.52 = (f32[4,5,1,32,2]{4,0,3,1,2:T(4,128)}, f32[4,5,1,32,2]{4,0,3,1,2:T(4,128)}) fusion(f32[4,5,1,32,256]{4,0,3,1,2:T(4,128)S(1)} %copy.48), kind=kLoop, calls=%fused_computation.109 | loop fusion | bytes 20480 | tf_op jit(solution)/shard_map/jit(_roll_static)/slice | solution.py:103
  47.5 1.1 %fusion.54 = (f32[4,5,1,32,1]{4,0,3,1,2:T(4,128)}, f32[4,5,1,32,1]{4,0,3,1,2:T(4,128)}) fusion(f32[4,5,1,32,256]{4,0,3,1,2:T(4,128)S(1)} %copy.48), kind=kLoop, calls=%fused_computation.111 | loop fusion | bytes 10240 | tf_op jit(solution)/shard_map/jit(_roll_static)/slice | solution.py:102
  51.3 0.6 iota_compare_fusion
  51.9 0.0 collective-permute-done
  51.9 0.0 collective-permute-done.1
  52.0 0.0 collective-permute-done.2
  52.0 0.0 collective-permute-done.3
  52.1 0.2 fusion.30
  52.3 0.2 fusion.29
  52.5 0.3 fusion.12
  52.8 0.7 slice_dynamic-update-slice_fusion
  53.5 0.8 add_dynamic-update-slice_fusion
  54.2 0.7 multiply_dynamic-update-slice_fusion.2
  54.9 0.7 multiply_dynamic-update-slice_fusion.1
  55.6 0.7 multiply_dynamic-update-slice_fusion
  56.4 29.0 %all-gather.2.cloned.1.call-done = f32[8,5,1,32,256]{4,3,2,1,0:T(8,128)} async-done(((f32[4,5,1,32,256]{4,3,2,1,0:T(8,128)}), f32[8,5,1,32,256]{4,3,2,1,0:T(8,128)}) %all-gather.2.cloned.1.call-update) | async-done | bytes 1310736 | tf_op jit(solution)/shard_map/all_gather | solution.py:138
  85.4 7.7 %fusion.9 = f32[4,5,1,32,256]{4,0,3,1,2:T(4,128)S(1)} fusion(f32[8,5,1,32,256]{4,3,2,1,0:T(8,128)} %all-gather.2.cloned.1.call-done, f32[4,5,1,36,256]{4,0,3,1,2:T(4,128)S(1)} %fusion.12, f32[4,5,1,36,256]{4,0,3,1,2:T(4,128)} %multiply_dynamic-update-slice_fusion, f32[4,5,1,32,1]{4,0,3,1,2:T(4,128)} %get-tuple-element.81, ...), kind=kOutput, calls=%fused_computation.7 | convolution fusion | flops 21954560 | bytes 13775364 | tf_op jit(solution)/shard_map/nm,mvbij->nvbij/dot_general | solution.py:139
  93.1 1.0 copy.64
  (35 shorter events, 0.4 us)
Async XLA Ops:
  6.5 22.0 %copy-start = (s32[256,2]{0,1:T(2,128)S(1)}, s32[256,2]{0,1:T(2,128)}, u32[]{:S(2)}) copy-start(s32[256,2]{0,1:T(2,128)} %param.10) | copy-start | bytes 6148
  6.5 22.2 %copy-start.1 = (s32[256]{0:T(256)S(1)}, s32[256]{0:T(256)}, u32[]{:S(2)}) copy-start(s32[256]{0:T(256)} %param.9) | copy-start | bytes 3076
  6.5 31.9 %copy-start.4 = (f32[4,5,1,32,256]{4,3,2,1,0:T(8,128)S(1)}, f32[4,5,1,32,256]{4,3,2,1,0:T(8,128)}, u32[]{:S(2)}) copy-start(f32[4,5,1,32,256]{4,3,2,1,0:T(8,128)} %param.8) | copy-start | bytes 1966084
  6.5 26.1 %copy-start.6 = (s32[256,2]{0,1:T(2,128)S(1)}, s32[256,2]{0,1:T(2,128)}, u32[]{:S(2)}) copy-start(s32[256,2]{0,1:T(2,128)} %param.11) | copy-start | bytes 6148
  6.5 26.1 %copy-start.5 = (s32[256,2]{0,1:T(2,128)S(1)}, s32[256,2]{0,1:T(2,128)}, u32[]{:S(2)}) copy-start(s32[256,2]{0,1:T(2,128)} %param.12) | copy-start | bytes 6148
  6.5 78.8 %all-gather.2.cloned.1.call-start = ((), (), s32[]{:S(2)}) async-start(), calls=%async_computation | async-start | bytes 1966080 | tf_op jit(solution)/shard_map/all_gather | solution.py:138
  15.2 36.7 %collective-permute-start = (f32[4,5,1,2,2,256]{5,4,1,0,3,2:T(2,128)S(1)}, f32[4,5,1,2,2,256]{5,4,1,0,3,2:T(2,128)S(1)}, u32[]{:S(2)}, u32[]{:S(2)}) collective-permute-start(f32[4,5,1,2,2,256]{5,4,1,0,3,2:T(2,128)S(1)} %pad_maximum_fusion), channel_id=1, source_target_pairs={{0,2},{1,3},{2,4},{3,5},{4,6},{5,7},{6,8},{7,9},{8,10},{9,11},{10,... | collective-permute-start | bytes 245768 | tf_op jit(solution)/shard_map/ppermute | solution.py:16
  18.4 33.5 %collective-permute-start.1 = (f32[4,5,1,2,2,256]{5,4,1,0,3,2:T(2,128)S(1)}, f32[4,5,1,2,2,256]{5,4,1,0,3,2:T(2,128)S(1)}, u32[]{:S(2)}, u32[]{:S(2)}) collective-permute-start(f32[4,5,1,2,2,256]{5,4,1,0,3,2:T(2,128)S(1)} %pad_maximum_fusion), channel_id=1, source_target_pairs={{0,1},{1,2},{2,3},{3,4},{4,5},{5,6},{6,7},{7,8},{8,9},{9,10},{10,1... | collective-permute-start | bytes 245768 | tf_op jit(solution)/shard_map/ppermute | solution.py:16
  22.3 29.7 %collective-permute-start.2 = (f32[4,5,1,2,2,256]{5,4,1,0,3,2:T(2,128)S(1)}, f32[4,5,1,2,2,256]{5,4,1,0,3,2:T(2,128)S(1)}, u32[]{:S(2)}, u32[]{:S(2)}) collective-permute-start(f32[4,5,1,2,2,256]{5,4,1,0,3,2:T(2,128)S(1)} %pad_maximum_fusion), channel_id=1, source_target_pairs={{0,255},{1,0},{2,1},{3,2},{4,3},{5,4},{6,5},{7,6},{8,7},{9,8},{10,... | collective-permute-start | bytes 245768 | tf_op jit(solution)/shard_map/ppermute | solution.py:16
  24.2 27.8 %collective-permute-start.3 = (f32[4,5,1,2,2,256]{5,4,1,0,3,2:T(2,128)S(1)}, f32[4,5,1,2,2,256]{5,4,1,0,3,2:T(2,128)S(1)}, u32[]{:S(2)}, u32[]{:S(2)}) collective-permute-start(f32[4,5,1,2,2,256]{5,4,1,0,3,2:T(2,128)S(1)} %pad_maximum_fusion), channel_id=1, source_target_pairs={{0,254},{1,255},{2,0},{3,1},{4,2},{5,3},{6,4},{7,5},{8,6},{9,7},{1... | collective-permute-start | bytes 245768 | tf_op jit(solution)/shard_map/ppermute | solution.py:16
  38.9 8.5 %copy-start.2 = (f32[4,5,1,32,256]{4,0,3,1,2:T(4,128)}, f32[4,5,1,32,256]{4,0,3,1,2:T(4,128)S(1)}, u32[]{:S(2)}) copy-start(f32[4,5,1,32,256]{4,0,3,1,2:T(4,128)S(1)} %copy.48) | copy-start | bytes 1966084
  48.5 4.0 %copy-start.3 = (f32[4,5,1,32,256]{4,0,3,1,2:T(4,128)S(1)}, f32[4,5,1,32,256]{4,0,3,1,2:T(4,128)}, u32[]{:S(2)}) copy-start(f32[4,5,1,32,256]{4,0,3,1,2:T(4,128)} %copy-done.2) | copy-start | bytes 1966084
  48.6 4.0 %slice-start = ((f32[4,5,1,32,256]{4,0,3,1,2:T(4,128)}), f32[4,5,1,2,256]{4,0,3,1,2:T(4,128)S(1)}, s32[]{:S(2)}) async-start(f32[4,5,1,32,256]{4,0,3,1,2:T(4,128)} %copy-done.2), calls=%async_computation.1 | async-start | bytes 81920 | tf_op jit(solution)/shard_map/slice | solution.py:72
Sparse Core Ops, SparseCore 0:
  28.7 56.6 all-gather.1
where the time goes:
time: 101 us
  waiting for transfers between devices  29 us (29%)
  between operations  26.1 us (26%)
  local copies, waits for them, and re-layouts  18.7 us (19%)
  starting transfers between devices  13.4 us (13%)
  matrix products  7.73 us (8%)
  other arithmetic  5.89 us (6%)
    all_gather x1, waiting for transfers between devices, on_device(): all_states = lax.all_gather(state, 'inst', axis=0, tiled=True)  29 us
    ppermute x4, starting transfers between devices, passed_along(): return lax.ppermute(value, axis, pairs)  13.3 us
    dot_general x1, matrix products, on_device(): jnp.einsum('nm,mvbij->nvbij', own_rows, all_states, precision=lax.Precisi...  7.73 us
    slice x2, local copies, waits for them, and re-layouts, spatial_residual(): jnp.roll(fields, 1, 4)  2.62 us
    slice x2, local copies, waits for them, and re-layouts, spatial_residual(): jnp.roll(fields, 2, 4)  2.58 us
    slice x2, local copies, waits for them, and re-layouts, spatial_residual(): jnp.roll(flux_cols, 1, 4)  2.56 us
    unnamed x7, other arithmetic  2.49 us
  transfers between devices with their start and end apart: 5, of which 1 were waited for; matrix products, arithmetic and copies ran while one was open for 18% of the time, Pallas kernels for 0%

commit v1 on v0

--- a/solution.py
+++ b/solution.py
@@ -135,7 +135,9 @@
     cycle_place = lax.axis_index("inst")
     derivative = spectral_matrix(inst_dev * cycle_size)
     own_rows = lax.dynamic_slice_in_dim(derivative, cycle_place * inst_dev, inst_dev, 0)
-    all_states = lax.all_gather(state, "inst", axis=0, tiled=True)
+    all_states = jnp.concatenate(
+        lax.all_to_all(jnp.stack([state] * lax.axis_size("inst")), "inst", 0, 0), axis=0
+    )
     source = jnp.einsum("nm,mvbij->nvbij", own_rows, all_states, precision=lax.Precision.HIGHEST)
     inside = (jnp.arange(row_count, dtype=jnp.int32)[None, :] < my_rows[:, None])[
         None, None, :, :, None

time: 101 us -> 77.6 us (0.77)
  the two profiles are of different devices: /device:TPU:9 before, /device:TPU:32 now
where the time goes in v1:
time: 77.6 us; the launch traced here: 77.1 us
  starting transfers between devices  28.4 us (37%)
  local copies, waits for them, and re-layouts  20 us (26%)
  between operations  12.7 us (16%)
  other arithmetic  8.64 us (11%)
  matrix products  7.41 us (10%)
    ppermute x4, starting transfers between devices, passed_along(): return lax.ppermute(value, axis, pairs)  21 us
    dot_general x1, matrix products, on_device(): jnp.einsum('nm,mvbij->nvbij', own_rows, all_states, precision=lax.Precisi...  7.41 us
    all_to_all x1, starting transfers between devices, on_device(): lax.all_to_all(jnp.stack([state] * lax.axis_size('inst')), 'inst', 0, 0)  7.33 us
    slice x2, local copies, waits for them, and re-layouts, spatial_residual(): jnp.roll(flux_cols, 2, 4)  2.62 us
    slice x2, local copies, waits for them, and re-layouts, spatial_residual(): jnp.roll(fields, 2, 4)  2.62 us
    slice x2, local copies, waits for them, and re-layouts, spatial_residual(): jnp.roll(flux_cols, 1, 4)  2.59 us
    slice x2, local copies, waits for them, and re-layouts, spatial_residual(): jnp.roll(fields, 1, 4)  2.54 us
    another operation x1, other arithmetic, on_device(): jnp.stack([state] * lax.axis_size('inst'))  2.54 us
  transfers between devices with their start and end apart: 5, of which 0 were waited for; matrix products, arithmetic and copies ran while one was open for 29% of the time, Pallas kernels for 0%

profile of v1, /device:TPU:32, one launch (start us, length us, event | category | flops | bytes accessed | tf_op | source)
XLA Modules:
  0.0 77.1 jit_solution(13649855710008456810)
XLA Ops:
  0.0 0.7 compare_select_fusion
  0.7 1.4 %scatter_custom_fusion = s32[256]{0:T(256)S(1)} fusion(s32[256]{0:T(256)S(1)} %compare_select_fusion, s32[256]{0:T(256)S(1)} %iota.25, s32[]{:T(128)} %constant.170.clone.1), kind=kCustom, calls=%fused_computation.104 | custom fusion | bytes 1028 | tf_op jit(solution)/shard_map/scatter | solution.py:114
  2.1 0.7 dynamic-slice.18
  4.8 1.3 %dynamic-slice.19 = s32[1]{0:T(128)} dynamic-slice(s32[256]{0:T(256)} %param.13, s32[]{:T(128)} %bitcast.2), dynamic_slice_sizes={1} | dynamic-slice | bytes 12 | tf_op jit(solution)/shard_map/gather | solution.py:119
  7.6 1.0 %slice_bitcast_fusion = (f32[4,5,1,1,2,256]{5,4,1,0,3,2:T(2,128)S(1)}, f32[4,5,2,256]{3,2,1,0:T(2,128)S(1)}) fusion(f32[4,5,1,32,256]{4,3,2,1,0:T(8,128)} %param.8, s32[]{:T(128)S(6)} %select_n.131), kind=kLoop, calls=%fused_computation.65 | loop fusion | bytes 163844 | tf_op jit(solution)/shard_map/stack | solution.py:57
  8.6 0.2 rev.6
  8.8 3.5 %collective-permute-start = (f32[4,5,1,2,2,256]{5,4,1,0,3,2:T(2,128)S(1)}, f32[4,5,1,2,2,256]{5,4,1,0,3,2:T(2,128)S(1)}, u32[]{:S(2)}, u32[]{:S(2)}) collective-permute-start(f32[4,5,1,2,2,256]{5,4,1,0,3,2:T(2,128)S(1)} %pad_maximum_fusion.1), channel_id=1, source_target_pairs={{0,2},{1,3},{2,4},{3,5},{4,6},{5,7},{6,8},{7,9},{8,10},{9,11},{10,... | collective-permute-start | bytes 245768 | tf_op jit(solution)/shard_map/ppermute | solution.py:16
  12.3 1.9 %collective-permute-start.1 = (f32[4,5,1,2,2,256]{5,4,1,0,3,2:T(2,128)S(1)}, f32[4,5,1,2,2,256]{5,4,1,0,3,2:T(2,128)S(1)}, u32[]{:S(2)}, u32[]{:S(2)}) collective-permute-start(f32[4,5,1,2,2,256]{5,4,1,0,3,2:T(2,128)S(1)} %pad_maximum_fusion.1), channel_id=1, source_target_pairs={{0,1},{1,2},{2,3},{3,4},{4,5},{5,6},{6,7},{7,8},{8,9},{9,10},{10,1... | collective-permute-start | bytes 245768 | tf_op jit(solution)/shard_map/ppermute | solution.py:16
  14.3 11.4 %collective-permute-start.2 = (f32[4,5,1,2,2,256]{5,4,1,0,3,2:T(2,128)S(1)}, f32[4,5,1,2,2,256]{5,4,1,0,3,2:T(2,128)S(1)}, u32[]{:S(2)}, u32[]{:S(2)}) collective-permute-start(f32[4,5,1,2,2,256]{5,4,1,0,3,2:T(2,128)S(1)} %pad_maximum_fusion.1), channel_id=1, source_target_pairs={{0,255},{1,0},{2,1},{3,2},{4,3},{5,4},{6,5},{7,6},{8,7},{9,8},{10,... | collective-permute-start | bytes 245768 | tf_op jit(solution)/shard_map/ppermute | solution.py:16
  25.7 4.2 %collective-permute-start.3 = (f32[4,5,1,2,2,256]{5,4,1,0,3,2:T(2,128)S(1)}, f32[4,5,1,2,2,256]{5,4,1,0,3,2:T(2,128)S(1)}, u32[]{:S(2)}, u32[]{:S(2)}) collective-permute-start(f32[4,5,1,2,2,256]{5,4,1,0,3,2:T(2,128)S(1)} %pad_maximum_fusion.1), channel_id=1, source_target_pairs={{0,254},{1,255},{2,0},{3,1},{4,2},{5,3},{6,4},{7,5},{8,6},{9,7},{1... | collective-permute-start | bytes 245768 | tf_op jit(solution)/shard_map/ppermute | solution.py:16
  29.9 2.5 %pad_maximum_fusion = f32[2,4,5,1,32,256]{5,4,2,1,3,0:T(8,128)} fusion(f32[1,4,5,1,32,256]{5,4,2,1,3,0:T(8,128)} %bitcast.52), kind=kLoop, calls=%fused_computation.2 | loop fusion | flops 327680 | bytes 1966080 | tf_op jit(solution)/shard_map/stack | solution.py:139
  32.5 7.3 %all-to-all-start = ((f32[2,4,5,1,32,256]{5,4,2,1,3,0:T(8,128)}), f32[2,4,5,1,32,256]{5,4,2,1,3,0:T(8,128)S(1)}, u32[]{:S(2)}, u32[]{:S(2)}) async-start(f32[2,4,5,1,32,256]{5,4,2,1,3,0:T(8,128)} %pad_maximum_fusion), calls=%async_computation | async-start | bytes 2621440 | tf_op jit(solution)/shard_map/all_to_all | solution.py:139
  39.8 0.4 copy.28
  40.2 0.0 copy-start.2
  40.3 0.1 constant_dynamic-slice_fusion
  40.3 0.7 fusion.60
  41.6 0.2 fusion.44
  41.8 0.6 gather_fusion
  42.5 0.6 fusion.61
  45.4 0.6 fusion.59
  49.4 0.7 fusion.49
  50.1 0.1 multiply_dynamic-update-slice_fusion.5
  50.2 0.1 add_dynamic-update-slice_fusion.1
  50.4 0.1 multiply_dynamic-update-slice_fusion.3
  50.4 1.1 %fusion.57 = (f32[4,5,1,32,1]{4,0,3,1,2:T(4,128)}, f32[4,5,1,32,1]{4,0,3,1,2:T(4,128)}) fusion(f32[4,5,1,32,256]{4,0,3,1,2:T(4,128)S(1)} %multiply_dynamic-update-slice_fusion.3), kind=kLoop, calls=%fused_computation.115 | loop fusion | bytes 10240 | tf_op jit(solution)/shard_map/jit(_roll_static)/slice | solution.py:95
  51.5 1.5 %fusion.58 = (f32[4,5,1,32,255]{4,0,3,1,2:T(4,128)}, f32[4,5,1,32,255]{4,0,3,1,2:T(4,128)}) fusion(f32[4,5,1,32,256]{4,0,3,1,2:T(4,128)S(1)} %multiply_dynamic-update-slice_fusion.3), kind=kLoop, calls=%fused_computation.116 | loop fusion | bytes 2611200 | tf_op jit(solution)/shard_map/jit(_roll_static)/slice | solution.py:95
  53.0 1.1 %fusion.55 = (f32[4,5,1,32,2]{4,0,3,1,2:T(4,128)}, f32[4,5,1,32,2]{4,0,3,1,2:T(4,128)}) fusion(f32[4,5,1,32,256]{4,0,3,1,2:T(4,128)S(1)} %multiply_dynamic-update-slice_fusion.3), kind=kLoop, calls=%fused_computation.113 | loop fusion | bytes 20480 | tf_op jit(solution)/shard_map/jit(_roll_static)/slice | solution.py:96
  54.1 1.5 %fusion.56 = (f32[4,5,1,32,254]{4,0,3,1,2:T(4,128)}, f32[4,5,1,32,254]{4,0,3,1,2:T(4,128)}) fusion(f32[4,5,1,32,256]{4,0,3,1,2:T(4,128)S(1)} %multiply_dynamic-update-slice_fusion.3), kind=kLoop, calls=%fused_computation.114 | loop fusion | bytes 2600960 | tf_op jit(solution)/shard_map/jit(_roll_static)/slice | solution.py:96
  55.7 1.1 %fusion.51 = (f32[4,5,1,32,2]{4,0,3,1,2:T(4,128)}, f32[4,5,1,32,2]{4,0,3,1,2:T(4,128)}) fusion(f32[4,5,1,32,256]{4,0,3,1,2:T(4,128)S(1)} %copy.28), kind=kLoop, calls=%fused_computation.109 | loop fusion | bytes 20480 | tf_op jit(solution)/shard_map/jit(_roll_static)/slice | solution.py:103
  56.7 1.5 %fusion.52 = (f32[4,5,1,32,254]{4,0,3,1,2:T(4,128)}, f32[4,5,1,32,254]{4,0,3,1,2:T(4,128)}) fusion(f32[4,5,1,32,256]{4,0,3,1,2:T(4,128)S(1)} %copy.28), kind=kLoop, calls=%fused_computation.110 | loop fusion | bytes 2600960 | tf_op jit(solution)/shard_map/jit(_roll_static)/slice | solution.py:103
  58.3 1.0 %fusion.53 = (f32[4,5,1,32,1]{4,0,3,1,2:T(4,128)}, f32[4,5,1,32,1]{4,0,3,1,2:T(4,128)}) fusion(f32[4,5,1,32,256]{4,0,3,1,2:T(4,128)S(1)} %copy.28), kind=kLoop, calls=%fused_computation.111 | loop fusion | bytes 10240 | tf_op jit(solution)/shard_map/jit(_roll_static)/slice | solution.py:102
  59.3 1.5 %fusion.54 = (f32[4,5,1,32,255]{4,0,3,1,2:T(4,128)}, f32[4,5,1,32,255]{4,0,3,1,2:T(4,128)}) fusion(f32[4,5,1,32,256]{4,0,3,1,2:T(4,128)S(1)} %copy.28), kind=kLoop, calls=%fused_computation.112 | loop fusion | bytes 2611200 | tf_op jit(solution)/shard_map/jit(_roll_static)/slice | solution.py:102
  63.5 0.7 iota_compare_fusion
  64.2 0.0 collective-permute-done
  64.2 0.0 collective-permute-done.1
  64.3 0.0 collective-permute-done.2
  64.3 0.0 collective-permute-done.3
  64.4 0.2 fusion.28
  64.6 0.2 fusion.29
  64.9 0.3 fusion.11
  65.1 0.7 slice_dynamic-update-slice_fusion
  65.8 0.8 %add_dynamic-update-slice_fusion = (f32[4,5,1,36,256]{4,0,3,1,2:T(4,128)}, f32[4,1,1,36,256]{4,0,3,1,2:T(4,128)S(1)}, f32[4,1,1,36,256]{4,0,3,1,2:T(4,128)S(1)}) fusion(f32[4,5,1,36,256]{4,0,3,1,2:T(4,128)} %slice_dynamic-update-slice_fusion, f32[4,5,1,36,256]{4,0,3,1,2:T(4,128)S(1)} %fusion.11), kind=kLoop, calls=%fused_computation.40 | loop fusion | flops 442368 | bytes 1179648
  66.6 0.7 multiply_dynamic-update-slice_fusion.2
  67.3 0.7 multiply_dynamic-update-slice_fusion.1
  68.0 0.7 multiply_dynamic-update-slice_fusion
  68.7 0.0 all-to-all-done
  68.7 7.4 %fusion.8 = f32[4,5,1,32,256]{4,0,3,1,2:T(4,128)S(1)} fusion(f32[8,5,32,256]{3,2,1,0:T(8,128)S(1)} %bitcast.53, f32[4,5,1,36,256]{4,0,3,1,2:T(4,128)S(1)} %fusion.11, f32[4,5,1,36,256]{4,0,3,1,2:T(4,128)} %multiply_dynamic-update-slice_fusion, f32[4,5,1,32,1]{4,0,3,1,2:T(4,128)} %get-tuple-element.81, f32[4,5,1,32,255]{4,0,3,1,2:T(4,128)} %get-tuple-element.83, ...), kind=kOutput, calls=%fused_computation.7 | convolution fusion | flops 21954560 | bytes 13765124 | tf_op jit(solution)/shard_map/nm,mvbij->nvbij/dot_general | solution.py:141
  76.1 1.0 %copy.44 = f32[4,5,1,32,256]{4,3,2,1,0:T(8,128)} copy(f32[4,5,1,32,256]{4,0,3,1,2:T(4,128)S(1)} %fusion.8) | data formatting | bytes 1310720 | tf_op jit(solution)/shard_map/jit(_where)/select_n | solution.py:145
  (35 shorter events, 0.4 us)
Async XLA Ops:
  0.0 41.6 %copy-start = (s32[256,2]{0,1:T(2,128)S(1)}, s32[256,2]{0,1:T(2,128)}, u32[]{:S(2)}) copy-start(s32[256,2]{0,1:T(2,128)} %param.10) | copy-start | bytes 6148
  8.8 55.3 %collective-permute-start = (f32[4,5,1,2,2,256]{5,4,1,0,3,2:T(2,128)S(1)}, f32[4,5,1,2,2,256]{5,4,1,0,3,2:T(2,128)S(1)}, u32[]{:S(2)}, u32[]{:S(2)}) collective-permute-start(f32[4,5,1,2,2,256]{5,4,1,0,3,2:T(2,128)S(1)} %pad_maximum_fusion.1), channel_id=1, source_target_pairs={{0,2},{1,3},{2,4},{3,5},{4,6},{5,7},{6,8},{7,9},{8,10},{9,11},{10,... | collective-permute-start | bytes 245768 | tf_op jit(solution)/shard_map/ppermute | solution.py:16
  12.3 51.9 %collective-permute-start.1 = (f32[4,5,1,2,2,256]{5,4,1,0,3,2:T(2,128)S(1)}, f32[4,5,1,2,2,256]{5,4,1,0,3,2:T(2,128)S(1)}, u32[]{:S(2)}, u32[]{:S(2)}) collective-permute-start(f32[4,5,1,2,2,256]{5,4,1,0,3,2:T(2,128)S(1)} %pad_maximum_fusion.1), channel_id=1, source_target_pairs={{0,1},{1,2},{2,3},{3,4},{4,5},{5,6},{6,7},{7,8},{8,9},{9,10},{10,1... | collective-permute-start | bytes 245768 | tf_op jit(solution)/shard_map/ppermute | solution.py:16
  14.3 50.0 %collective-permute-start.2 = (f32[4,5,1,2,2,256]{5,4,1,0,3,2:T(2,128)S(1)}, f32[4,5,1,2,2,256]{5,4,1,0,3,2:T(2,128)S(1)}, u32[]{:S(2)}, u32[]{:S(2)}) collective-permute-start(f32[4,5,1,2,2,256]{5,4,1,0,3,2:T(2,128)S(1)} %pad_maximum_fusion.1), channel_id=1, source_target_pairs={{0,255},{1,0},{2,1},{3,2},{4,3},{5,4},{6,5},{7,6},{8,7},{9,8},{10,... | collective-permute-start | bytes 245768 | tf_op jit(solution)/shard_map/ppermute | solution.py:16
  25.7 38.6 %collective-permute-start.3 = (f32[4,5,1,2,2,256]{5,4,1,0,3,2:T(2,128)S(1)}, f32[4,5,1,2,2,256]{5,4,1,0,3,2:T(2,128)S(1)}, u32[]{:S(2)}, u32[]{:S(2)}) collective-permute-start(f32[4,5,1,2,2,256]{5,4,1,0,3,2:T(2,128)S(1)} %pad_maximum_fusion.1), channel_id=1, source_target_pairs={{0,254},{1,255},{2,0},{3,1},{4,2},{5,3},{6,4},{7,5},{8,6},{9,7},{1... | collective-permute-start | bytes 245768 | tf_op jit(solution)/shard_map/ppermute | solution.py:16
  32.5 7.3 %copy-start.4 = (f32[4,5,1,32,256]{4,3,2,1,0:T(8,128)S(1)}, f32[4,5,1,32,256]{4,3,2,1,0:T(8,128)}, u32[]{:S(2)}) copy-start(f32[4,5,1,32,256]{4,3,2,1,0:T(8,128)} %param.8) | copy-start | bytes 1966084
  32.5 7.8 %copy-start.5 = (s32[256,2]{0,1:T(2,128)S(1)}, s32[256,2]{0,1:T(2,128)}, u32[]{:S(2)}) copy-start(s32[256,2]{0,1:T(2,128)} %param.12) | copy-start | bytes 6148
  32.5 7.8 %copy-start.6 = (s32[256,2]{0,1:T(2,128)S(1)}, s32[256,2]{0,1:T(2,128)}, u32[]{:S(2)}) copy-start(s32[256,2]{0,1:T(2,128)} %param.11) | copy-start | bytes 6148
  32.5 36.2 %all-to-all-start = ((f32[2,4,5,1,32,256]{5,4,2,1,3,0:T(8,128)}), f32[2,4,5,1,32,256]{5,4,2,1,3,0:T(8,128)S(1)}, u32[]{:S(2)}, u32[]{:S(2)}) async-start(f32[2,4,5,1,32,256]{5,4,2,1,3,0:T(8,128)} %pad_maximum_fusion), calls=%async_computation | async-start | bytes 2621440 | tf_op jit(solution)/shard_map/all_to_all | solution.py:139
  39.8 2.0 %copy-start.1 = (s32[256]{0:T(256)S(1)}, s32[256]{0:T(256)}, u32[]{:S(2)}) copy-start(s32[256]{0:T(256)} %param.9) | copy-start | bytes 3076
  40.2 19.1 %copy-start.2 = (f32[4,5,1,32,256]{4,0,3,1,2:T(4,128)}, f32[4,5,1,32,256]{4,0,3,1,2:T(4,128)S(1)}, u32[]{:S(2)}) copy-start(f32[4,5,1,32,256]{4,0,3,1,2:T(4,128)S(1)} %copy.28) | copy-start | bytes 1966084
  60.8 4.0 %copy-start.3 = (f32[4,5,1,32,256]{4,0,3,1,2:T(4,128)S(1)}, f32[4,5,1,32,256]{4,0,3,1,2:T(4,128)}, u32[]{:S(2)}) copy-start(f32[4,5,1,32,256]{4,0,3,1,2:T(4,128)} %copy-done.2) | copy-start | bytes 1966084
  60.8 4.0 %slice-start = ((f32[4,5,1,32,256]{4,0,3,1,2:T(4,128)}), f32[4,5,1,2,256]{4,0,3,1,2:T(4,128)S(1)}, s32[]{:S(2)}) async-start(f32[4,5,1,32,256]{4,0,3,1,2:T(4,128)} %copy-done.2), calls=%async_computation.1 | async-start | bytes 81920 | tf_op jit(solution)/shard_map/slice | solution.py:72
